TPU v7x, 512 devices: a whole 4x4x16 slice. The times are simulated.
512 devices in a mesh: dp: 64 (over z, x), tensor: 8 (over y, core).
Axes of the slice: x: 4, y: 4, z: 16, core: 2. Of those that a mesh axis runs over, the one named last changes fastest.
Arguments:
- queries: bfloat16 [4096, 8, 32, 128], P('dp', None, 'tensor'), may hold values from -8 to 8
- keys_new: bfloat16 [4096, 8, 8, 128], P('dp', None, 'tensor'), may hold values from -6 to 6
- values_new: bfloat16 [4096, 8, 8, 128], P('dp', None, 'tensor'), may hold values from -6 to 6
- residual: bfloat16 [4096, 8, 4096], P('dp', None, 'tensor'), may hold values from -4 to 4
- cand_len: int32 [4096], P('dp'), may hold values from 1 to 8, as said below
- owner_map: int32 [4096], P('dp'), may hold values from 0 to 63, as said below
- prompt_len: int32 [64], P('dp'), may hold values from 2 to 2048, as said below
- keys_cache: bfloat16 [64, 2048, 8, 128], P('dp', None, 'tensor'), may hold values from -6 to 6
- values_cache: bfloat16 [64, 2048, 8, 128], P('dp', None, 'tensor'), may hold values from -6 to 6
- norm_gain: bfloat16 [4096], P('tensor'), may hold values from 0.099609375 to 1.8984375
- value_head: bfloat16 [4096], P('tensor'), may hold values from -0.09375 to 0.09375
Outputs:
- values: float32 [4096, 8], P('dp')
Inputs may be any that keep to these rules, and one draw needn't show every extreme that they name: `owner_map`: at most 2 of the 64 candidates held by one dp index share a prompt; each prompt has at most 128 candidates in all, and some prompt has exactly 128, 2 from every dp index. `cand_len`: token slots at or past a candidate's length are padding; some candidate has all 8. `prompt_len`: cache rows at or past a prompt's length are unused; some prompt has all 2048.
All inputs are finite; a program needn't handle non-finite values.
Results may differ from a plain program's by a relative error of at most 0.0032.
Values may be sent and summed in bfloat16 or wider, within the bound.
A program may use at most 64 MiB of HBM per device.

v0:
```python
import math

import jax
import jax.numpy as jnp
from jax import lax
from jax.sharding import PartitionSpec as P

EPSILON = 1e-05


def pick_rows(source, index_rows, keep_mask):
    taken_rows = jnp.take(source, index_rows, axis=0)
    shaped = keep_mask.reshape(keep_mask.shape + (1,) * (taken_rows.ndim - 1))
    return jnp.where(shaped, taken_rows, jnp.zeros_like(taken_rows))


def attend(query_rows, key_rows, value_rows, cache_keys, cache_values, prompt_size, group_size):
    cand_count, length, feat_width = query_rows.shape
    prefix, kv_heads, head_dim = cache_keys.shape
    scaling = 1.0 / math.sqrt(head_dim)
    per_block = 1
    while cand_count % (per_block * 2) == 0 and per_block * length * kv_heads * group_size < 512:
        per_block = per_block * 2
    blocks = cand_count // per_block
    block_queries = query_rows.reshape(blocks, per_block, length, kv_heads, group_size, head_dim)
    block_keys = key_rows.reshape(blocks, per_block, length, kv_heads, head_dim)
    block_values = value_rows.reshape(blocks, per_block, length, kv_heads, head_dim)
    prefix_mask = jnp.arange(prefix, dtype=jnp.int32) < prompt_size
    causal = jnp.arange(length)[:, None] >= jnp.arange(length)[None, :]

    def one_block(operands):
        these_queries, these_keys, these_values = operands
        prefix_scores = (
            jnp.einsum(
                "clkgd,pkd->ckglp", these_queries, cache_keys, preferred_element_type=jnp.float32
            )
            * scaling
        )
        prefix_scores = jnp.where(prefix_mask, prefix_scores, -jnp.inf)
        own_scores = (
            jnp.einsum(
                "clkgd,cmkd->ckglm", these_queries, these_keys, preferred_element_type=jnp.float32
            )
            * scaling
        )
        own_scores = jnp.where(causal, own_scores, -jnp.inf)
        highest = jnp.maximum(jnp.max(prefix_scores, axis=-1), jnp.max(own_scores, axis=-1))
        exp_prefix = jnp.exp(prefix_scores - highest[..., None])
        exp_own = jnp.exp(own_scores - highest[..., None])
        denominator = jnp.sum(exp_prefix, axis=-1) + jnp.sum(exp_own, axis=-1)
        weight_prefix = (exp_prefix / denominator[..., None]).astype(jnp.bfloat16)
        weight_own = (exp_own / denominator[..., None]).astype(jnp.bfloat16)
        mixed_heads = jnp.einsum(
            "ckglp,pkd->clkgd", weight_prefix, cache_values, preferred_element_type=jnp.float32
        )
        mixed_heads = mixed_heads + jnp.einsum(
            "ckglm,cmkd->clkgd", weight_own, these_values, preferred_element_type=jnp.float32
        )
        return mixed_heads.astype(jnp.bfloat16).reshape(per_block, length, feat_width)

    mixed_heads = lax.map(one_block, (block_queries, block_keys, block_values))
    return mixed_heads.reshape(cand_count, length, feat_width)


def finish(mixed_heads, hidden_rows, lengths, norm_gain, value_head):
    cand_count, length, local_width = hidden_rows.shape
    hidden = hidden_rows.astype(jnp.float32) + mixed_heads.astype(jnp.float32)
    weight = norm_gain.astype(jnp.float32) * value_head.astype(jnp.float32)
    squares, dotted = lax.psum(
        (jnp.sum(hidden * hidden, axis=-1), jnp.sum(hidden * weight, axis=-1)), "tensor"
    )
    full_width = local_width * lax.axis_size("tensor")
    scored = dotted * lax.rsqrt(squares / full_width + EPSILON)
    inside = jnp.arange(length, dtype=jnp.int32)[None, :] < lengths[:, None]
    return jnp.where(inside, scored, jnp.zeros_like(scored))


def body(
    queries,
    keys_new,
    values_new,
    residual,
    cand_len,
    owner_map,
    prompt_len,
    keys_cache,
    values_cache,
    norm_gain,
    value_head,
):
    cand_count, length, local_heads, head_dim = queries.shape
    kv_local = keys_new.shape[2]
    group_size = local_heads // kv_local
    groups = lax.axis_size("dp")
    query_flat = queries.reshape(cand_count, length, local_heads * head_dim)
    key_flat = keys_new.reshape(cand_count, length, kv_local * head_dim)
    value_flat = values_new.reshape(cand_count, length, kv_local * head_dim)
    targets = jnp.arange(groups, dtype=jnp.int32)
    matches = owner_map[None, :] == targets[:, None]
    ranks = jnp.cumsum(matches.astype(jnp.int32), axis=1) - 1
    slot_ids = jnp.arange(2, dtype=jnp.int32)
    hits = matches[:, None, :] & (ranks[:, None, :] == slot_ids[None, :, None])
    cand_ids = jnp.arange(cand_count, dtype=jnp.int32)
    chosen = jnp.sum(jnp.where(hits, cand_ids[None, None, :], 0), axis=2).reshape(groups * 2)
    present = jnp.any(hits, axis=2).reshape(groups * 2)
    slot_pos = (2 * targets[:, None] + slot_ids[None, :])[:, :, None]
    back_pos = jnp.sum(jnp.where(hits, slot_pos, 0), axis=(0, 1))
    slot_len = jnp.where(present, jnp.take(cand_len, chosen), 0).astype(jnp.bfloat16)
    slot_queries = pick_rows(query_flat, chosen, present)
    slot_keys = pick_rows(key_flat, chosen, present)
    slot_values = pick_rows(value_flat, chosen, present)
    cache_keys = keys_cache[0]
    cache_values = values_cache[0]
    prompt_size = prompt_len[0]
    slot_hidden = pick_rows(residual, chosen, present)
    arrived = (
        lax.all_to_all(slot_queries, "dp", split_axis=0, concat_axis=0, tiled=True),
        lax.all_to_all(slot_keys, "dp", split_axis=0, concat_axis=0, tiled=True),
        lax.all_to_all(slot_values, "dp", split_axis=0, concat_axis=0, tiled=True),
        lax.all_to_all(slot_hidden, "dp", split_axis=0, concat_axis=0, tiled=True),
        lax.all_to_all(slot_len, "dp", split_axis=0, concat_axis=0, tiled=True),
    )
    arrived_len = arrived[4].astype(jnp.int32)
    mixed_heads = attend(
        arrived[0], arrived[1], arrived[2], cache_keys, cache_values, prompt_size, group_size
    )
    scored = finish(mixed_heads, arrived[3], arrived_len, norm_gain, value_head)
    homeward = lax.all_to_all(scored, "dp", split_axis=0, concat_axis=0, tiled=True)
    return jnp.take(homeward, back_pos, axis=0)


def solution(mesh):
    in_specs = (
        P("dp", None, "tensor", None),
        P("dp", None, "tensor", None),
        P("dp", None, "tensor", None),
        P("dp", None, "tensor"),
        P("dp"),
        P("dp"),
        P("dp"),
        P("dp", None, "tensor", None),
        P("dp", None, "tensor", None),
        P("tensor"),
        P("tensor"),
    )
    out_specs = P("dp", None)
    return jax.shard_map(body, mesh=mesh, in_specs=in_specs, out_specs=out_specs, check_vma=False)
```

profile of v0, /device:TPU:2, one launch (start us, length us, event | category | flops | bytes accessed | tf_op | source)
XLA Modules:
  0.0 259.7 jit_solution(12010665968696144770)
XLA Ops:
  0.0 0.8 iota_compare_fusion.4
  1.6 1.6 gather_fusion
  4.1 18.6 %all-to-all-start = ((bf16[64,2,1]{1,2,0:T(2,128)(2,1)}), bf16[64,2,1]{1,2,0:T(2,128)(2,1)S(1)}, u32[]{:S(2)}, u32[]{:S(2)}) async-start(bf16[64,2,1]{1,2,0:T(2,128)(2,1)} %copy.33), calls=%async_computation | async-start | bytes 65536 | tf_op jit(solution)/shard_map/all_to_all | solution.py:121
  23.2 1.6 gather_fusion.5
  24.8 1.6 gather_fusion.4
  26.4 1.1 select_select_fusion.2
  27.4 9.1 %all-to-all-done = bf16[64,2,1]{1,2,0:T(2,128)(2,1)S(1)} async-done(((bf16[64,2,1]{1,2,0:T(2,128)(2,1)}), bf16[64,2,1]{1,2,0:T(2,128)(2,1)S(1)}, u32[]{:S(2)}, u32[]{:S(2)}) %all-to-all-start) | async-done | bytes 288 | tf_op jit(solution)/shard_map/all_to_all | solution.py:121
  36.5 27.1 %all_to_all.38 = bf16[128,8,128]{2,1,0:T(8,128)(2,1)} all-to-all(bf16[128,8,128]{2,1,0:T(8,128)(2,1)S(1)} %get-tuple-element.103), channel_id=1, replica_groups=mesh['dp'=64,'tensor'=8] {'dp'}, dimensions={0} | all-to-all | bytes 524288 | tf_op jit(solution)/shard_map/all_to_all | solution.py:119
  63.6 5.7 %all-to-all-start.3 = ((bf16[128,8,128]{2,1,0:T(8,128)(2,1)}), bf16[128,8,128]{2,1,0:T(8,128)(2,1)S(1)}, u32[]{:S(2)}, u32[]{:S(2)}) async-start(bf16[128,8,128]{2,1,0:T(8,128)(2,1)} %get-tuple-element.104), calls=%async_computation.3 | async-start | bytes 524288 | tf_op jit(solution)/shard_map/all_to_all | solution.py:118
  70.8 1.7 select_select_fusion.1
  72.6 17.6 %all-to-all-done.3 = bf16[128,8,128]{2,1,0:T(8,128)(2,1)S(1)} async-done(((bf16[128,8,128]{2,1,0:T(8,128)(2,1)}), bf16[128,8,128]{2,1,0:T(8,128)(2,1)S(1)}, u32[]{:S(2)}, u32[]{:S(2)}) %all-to-all-start.3) | async-done | bytes 262176 | tf_op jit(solution)/shard_map/all_to_all | solution.py:118
  90.1 5.6 %all-to-all-start.2 = ((bf16[128,8,512]{2,1,0:T(8,128)(2,1)}), bf16[128,8,512]{2,1,0:T(8,128)(2,1)S(1)}, u32[]{:S(2)}, u32[]{:S(2)}) async-start(bf16[128,8,512]{2,1,0:T(8,128)(2,1)} %get-tuple-element.102), calls=%async_computation.2 | async-start | bytes 2097152 | tf_op jit(solution)/shard_map/all_to_all | solution.py:117
  96.1 54.0 %all-to-all-done.2 = bf16[128,8,512]{2,1,0:T(8,128)(2,1)S(1)} async-done(((bf16[128,8,512]{2,1,0:T(8,128)(2,1)}), bf16[128,8,512]{2,1,0:T(8,128)(2,1)S(1)}, u32[]{:S(2)}, u32[]{:S(2)}) %all-to-all-start.2) | async-done | bytes 1048608 | tf_op jit(solution)/shard_map/all_to_all | solution.py:117
  150.1 6.0 %all-to-all-start.1 = ((bf16[128,8,512]{2,1,0:T(8,128)(2,1)}), bf16[128,8,512]{2,1,0:T(8,128)(2,1)S(1)}, u32[]{:S(2)}, u32[]{:S(2)}) async-start(bf16[128,8,512]{2,1,0:T(8,128)(2,1)} %get-tuple-element.101), calls=%async_computation.1 | async-start | bytes 2097152 | tf_op jit(solution)/shard_map/all_to_all | solution.py:120
  156.0 45.7 %while.11 = (s32[]{:T(128)}, bf16[8,16,8,512]{3,2,1,0:T(8,128)(2,1)}, bf16[8,16,8,1,4,128]{5,2,4,1,3,0:T(8,128)(2,1)S(1)}, bf16[2048,1,128]{2,0,1:T(8,128)(2,1)S...) while((s32[]{:T(128)}, ...), condition=%wide.region_9.12_spmd.clone, body=%wide.region_4.11_spmd.clone.sunk | while | flops 547521600 | bytes 16799952 | solution.py:61
  157.5 0.8 fusion.63
  158.4 0.7 fusion.64
  159.2 1.0 convolution_bitcast_fusion.2
  160.2 1.6 fusion.66
  163.2 0.8 fusion.63
  164.1 0.7 fusion.64
  164.9 1.0 convolution_bitcast_fusion.2
  165.9 1.6 fusion.66
  168.9 0.8 fusion.63
  169.9 0.7 fusion.64
  170.6 1.0 convolution_bitcast_fusion.2
  171.6 1.6 fusion.66
  174.6 0.8 fusion.63
  175.6 0.7 fusion.64
  176.3 1.0 convolution_bitcast_fusion.2
  177.4 1.6 fusion.66
  180.3 0.8 fusion.63
  182.0 1.0 convolution_bitcast_fusion.2
  183.1 1.6 fusion.66
  186.0 0.8 fusion.63
  187.7 1.0 convolution_bitcast_fusion.2
  188.8 1.6 fusion.66
  191.7 0.8 fusion.63
  193.5 1.0 convolution_bitcast_fusion.2
  194.5 1.6 fusion.66
  197.4 0.8 fusion.63
  199.2 1.0 convolution_bitcast_fusion.2
  200.2 1.6 fusion.66
  201.8 7.7 %all-to-all-done.1 = bf16[128,8,512]{2,1,0:T(8,128)(2,1)S(1)} async-done(((bf16[128,8,512]{2,1,0:T(8,128)(2,1)}), bf16[128,8,512]{2,1,0:T(8,128)(2,1)S(1)}, u32[]{:S(2)}, u32[]{:S(2)}) %all-to-all-start.1) | async-done | bytes 1048608 | tf_op jit(solution)/shard_map/all_to_all | solution.py:120
  209.5 1.8 multiply_reduce_fusion
  211.3 24.9 %all-reduce = (f32[128,8]{1,0:T(8,128)S(1)}, f32[128,8]{1,0:T(8,128)S(1)}) all-reduce(f32[128,8]{1,0:T(8,128)S(1)} %get-tuple-element.76, f32[128,8]{1,0:T(8,128)S(1)} %get-tuple-element.75), channel_id=1, replica_groups=mesh['dp'=64,'tensor'=8] {'tensor'}, use_global_device_ids=true, to_apply=%region_11.14 | all-reduce | flops 2048 | bytes 16384 | tf_op jit(solution)/shard_map/psum | solution.py:69
  236.9 7.4 %all-to-all-start.5 = ((f32[64,2,8]{2,1,0:T(2,128)}), f32[64,2,8]{2,1,0:T(2,128)S(1)}, u32[]{:S(2)}, u32[]{:S(2)}) async-start(f32[64,2,8]{2,1,0:T(2,128)} %bitcast.12), calls=%async_computation.5 | async-start | bytes 131072 | tf_op jit(solution)/shard_map/all_to_all | solution.py:128
  244.3 14.1 %all-to-all-done.5 = f32[64,2,8]{2,1,0:T(2,128)S(1)} async-done(((f32[64,2,8]{2,1,0:T(2,128)}), f32[64,2,8]{2,1,0:T(2,128)S(1)}, u32[]{:S(2)}, u32[]{:S(2)}) %all-to-all-start.5) | async-done | bytes 4128 | tf_op jit(solution)/shard_map/all_to_all | solution.py:128
  (112 shorter events, 21.0 us)
Async XLA Ops:
  0.0 70.1 %copy-start = (bf16[64,8,512]{2,1,0:T(8,128)(2,1)S(1)}, bf16[64,8,512]{2,1,0:T(8,128)(2,1)}, u32[]{:S(2)}) copy-start(bf16[64,8,512]{2,1,0:T(8,128)(2,1)} %param.20) | copy-start | bytes 1572868
  0.0 69.3 %copy-start.2 = (bf16[64,8,4,128]{3,2,1,0:T(4,128)(2,1)S(1)}, bf16[64,8,4,128]{3,2,1,0:T(4,128)(2,1)}, u32[]{:S(2)}) copy-start(bf16[64,8,4,128]{3,2,1,0:T(4,128)(2,1)} %param.17) | copy-start | bytes 1572868
  4.1 32.4 %all-to-all-start = ((bf16[64,2,1]{1,2,0:T(2,128)(2,1)}), bf16[64,2,1]{1,2,0:T(2,128)(2,1)S(1)}, u32[]{:S(2)}, u32[]{:S(2)}) async-start(bf16[64,2,1]{1,2,0:T(2,128)(2,1)} %copy.33), calls=%async_computation | async-start | bytes 65536 | tf_op jit(solution)/shard_map/all_to_all | solution.py:121
  63.6 26.5 %all-to-all-start.3 = ((bf16[128,8,128]{2,1,0:T(8,128)(2,1)}), bf16[128,8,128]{2,1,0:T(8,128)(2,1)S(1)}, u32[]{:S(2)}, u32[]{:S(2)}) async-start(bf16[128,8,128]{2,1,0:T(8,128)(2,1)} %get-tuple-element.104), calls=%async_computation.3 | async-start | bytes 524288 | tf_op jit(solution)/shard_map/all_to_all | solution.py:118
  70.1 25.7 %copy-start.3 = (bf16[512]{0:T(512)(128)(2,1)S(1)}, bf16[512]{0:T(512)(128)(2,1)}, u32[]{:S(2)}) copy-start(bf16[512]{0:T(512)(128)(2,1)} %param.27) | copy-start | bytes 3076
  70.2 25.7 %copy-start.4 = (bf16[512]{0:T(512)(128)(2,1)S(1)}, bf16[512]{0:T(512)(128)(2,1)}, u32[]{:S(2)}) copy-start(bf16[512]{0:T(512)(128)(2,1)} %param.26) | copy-start | bytes 3076
  70.8 85.2 %copy-start.1 = (bf16[1,2048,1,128]{3,1,2,0:T(8,128)(2,1)S(1)}, bf16[1,2048,1,128]{3,1,2,0:T(8,128)(2,1)}, u32[]{:S(2)}) copy-start(bf16[1,2048,1,128]{3,1,2,0:T(8,128)(2,1)} %param.24) | copy-start | bytes 1572868
  90.1 59.9 %all-to-all-start.2 = ((bf16[128,8,512]{2,1,0:T(8,128)(2,1)}), bf16[128,8,512]{2,1,0:T(8,128)(2,1)S(1)}, u32[]{:S(2)}, u32[]{:S(2)}) async-start(bf16[128,8,512]{2,1,0:T(8,128)(2,1)} %get-tuple-element.102), calls=%async_computation.2 | async-start | bytes 2097152 | tf_op jit(solution)/shard_map/all_to_all | solution.py:117
  150.1 59.4 %all-to-all-start.1 = ((bf16[128,8,512]{2,1,0:T(8,128)(2,1)}), bf16[128,8,512]{2,1,0:T(8,128)(2,1)S(1)}, u32[]{:S(2)}, u32[]{:S(2)}) async-start(bf16[128,8,512]{2,1,0:T(8,128)(2,1)} %get-tuple-element.101), calls=%async_computation.1 | async-start | bytes 2097152 | tf_op jit(solution)/shard_map/all_to_all | solution.py:120
  157.4 2.8 %copy-start.5 = (bf16[2048,1,128]{2,0,1:T(8,128)(2,1)S(1)}, bf16[2048,1,128]{2,0,1:T(8,128)(2,1)}, u32[]{:S(2)}) copy-start(bf16[2048,1,128]{2,0,1:T(8,128)(2,1)} %get-tuple-element.187) | copy-start | bytes 1572868 | tf_op jit(solution)/shard_map/while
  163.2 2.8 %copy-start.5 = (bf16[2048,1,128]{2,0,1:T(8,128)(2,1)S(1)}, bf16[2048,1,128]{2,0,1:T(8,128)(2,1)}, u32[]{:S(2)}) copy-start(bf16[2048,1,128]{2,0,1:T(8,128)(2,1)} %get-tuple-element.187) | copy-start | bytes 1572868 | tf_op jit(solution)/shard_map/while
  168.9 2.8 %copy-start.5 = (bf16[2048,1,128]{2,0,1:T(8,128)(2,1)S(1)}, bf16[2048,1,128]{2,0,1:T(8,128)(2,1)}, u32[]{:S(2)}) copy-start(bf16[2048,1,128]{2,0,1:T(8,128)(2,1)} %get-tuple-element.187) | copy-start | bytes 1572868 | tf_op jit(solution)/shard_map/while
  174.6 2.8 %copy-start.5 = (bf16[2048,1,128]{2,0,1:T(8,128)(2,1)S(1)}, bf16[2048,1,128]{2,0,1:T(8,128)(2,1)}, u32[]{:S(2)}) copy-start(bf16[2048,1,128]{2,0,1:T(8,128)(2,1)} %get-tuple-element.187) | copy-start | bytes 1572868 | tf_op jit(solution)/shard_map/while
  180.3 2.8 %copy-start.5 = (bf16[2048,1,128]{2,0,1:T(8,128)(2,1)S(1)}, bf16[2048,1,128]{2,0,1:T(8,128)(2,1)}, u32[]{:S(2)}) copy-start(bf16[2048,1,128]{2,0,1:T(8,128)(2,1)} %get-tuple-element.187) | copy-start | bytes 1572868 | tf_op jit(solution)/shard_map/while
  186.0 2.8 %copy-start.5 = (bf16[2048,1,128]{2,0,1:T(8,128)(2,1)S(1)}, bf16[2048,1,128]{2,0,1:T(8,128)(2,1)}, u32[]{:S(2)}) copy-start(bf16[2048,1,128]{2,0,1:T(8,128)(2,1)} %get-tuple-element.187) | copy-start | bytes 1572868 | tf_op jit(solution)/shard_map/while
  191.7 2.8 %copy-start.5 = (bf16[2048,1,128]{2,0,1:T(8,128)(2,1)S(1)}, bf16[2048,1,128]{2,0,1:T(8,128)(2,1)}, u32[]{:S(2)}) copy-start(bf16[2048,1,128]{2,0,1:T(8,128)(2,1)} %get-tuple-element.187) | copy-start | bytes 1572868 | tf_op jit(solution)/shard_map/while
  197.4 2.8 %copy-start.5 = (bf16[2048,1,128]{2,0,1:T(8,128)(2,1)S(1)}, bf16[2048,1,128]{2,0,1:T(8,128)(2,1)}, u32[]{:S(2)}) copy-start(bf16[2048,1,128]{2,0,1:T(8,128)(2,1)} %get-tuple-element.187) | copy-start | bytes 1572868 | tf_op jit(solution)/shard_map/while
  236.9 21.5 %all-to-all-start.5 = ((f32[64,2,8]{2,1,0:T(2,128)}), f32[64,2,8]{2,1,0:T(2,128)S(1)}, u32[]{:S(2)}, u32[]{:S(2)}) async-start(f32[64,2,8]{2,1,0:T(2,128)} %bitcast.12), calls=%async_computation.5 | async-start | bytes 131072 | tf_op jit(solution)/shard_map/all_to_all | solution.py:128
where the time goes:
time: 261 us; the launch traced here: 260 us
  waiting for transfers between devices  102 us (39%)
  blocking collectives  52 us (20%)
  starting transfers between devices  43.2 us (17%)
  matrix products  33 us (13%)
  other arithmetic  19.2 us (7%)
  local copies, waits for them, and re-layouts  9.27 us (4%)
    all_to_all x1, waiting for transfers between devices, body(): lax.all_to_all(slot_queries, 'dp', split_axis=0, concat_axis=0, tiled=True)  54 us
    all_to_all x1, blocking collectives, body(): lax.all_to_all(slot_values, 'dp', split_axis=0, concat_axis=0, tiled=True)  27.1 us
    psum x1, blocking collectives, finish(): lax.psum((jnp.sum(hidden * hidden, axis=-1), jnp.sum(hidden * weight, axi...  24.9 us
    all_to_all x1, starting transfers between devices, body(): lax.all_to_all(slot_len, 'dp', split_axis=0, concat_axis=0, tiled=True)  18.6 us
    all_to_all x1, waiting for transfers between devices, body(): lax.all_to_all(slot_keys, 'dp', split_axis=0, concat_axis=0, tiled=True)  17.6 us
    all_to_all x1, waiting for transfers between devices, body(): lax.all_to_all(scored, 'dp', split_axis=0, concat_axis=0, tiled=True)  14.1 us
    dot_general x8, matrix products, one_block(): jnp.einsum('ckglp,pkd->clkgd', weight_prefix, cache_values, preferred_ele...  12.5 us
    all_to_all x1, waiting for transfers between devices, body(): lax.all_to_all(slot_len, 'dp', split_axis=0, concat_axis=0, tiled=True)  9.11 us
  transfers between devices with their start and end apart: 5, of which 5 were waited for; matrix products, arithmetic and copies ran while one was open for 21% of the time, Pallas kernels for 0%

commit v1 on v0

v1 whole, which is shorter than its diff:
```python
import functools
import math

import jax
import jax.numpy as jnp
from jax import lax
from jax.experimental import pallas as pl
from jax.experimental.pallas import tpu as pltpu
from jax.sharding import PartitionSpec as P

EPSILON = 1e-05
MESH = pl.DeviceIdType.MESH
NZ = 16
NX = 4
NT = 8
RANKS = 2
GROUPS = NZ
PAIR = NX * RANKS
SLOTS = GROUPS * PAIR
LENGTH = 8
HEADS = 4
ROWS = HEADS * LENGTH
HD = 128
PMAX = 2048
CANDS = 64
FEATURES = 4096
MASKED = -1e30
LOG2E = math.log2(math.e)


def iota(shape, dim):
    return lax.broadcasted_iota(jnp.int32, shape, dim)


def group_dz(group):
    size = 8 - (group + 1) // 2
    return lax.rem(NZ + (2 * lax.rem(group, 2) - 1) * size, NZ)


def kernel(
    owner_ref,
    len_ref,
    weight_ref,
    plen_ref,
    q_hbm,
    kn_hbm,
    vn_hbm,
    res_hbm,
    kc_hbm,
    vc_hbm,
    out_ref,
    q_in,
    kn,
    vn,
    res,
    kc,
    vc,
    q_perm,
    q_out,
    q_got,
    m_out,
    m_got,
    l_out,
    l_got,
    own_o,
    own_l,
    bias,
    idx_v,
    idx_s,
    place,
    acc,
    part,
    load_sem,
    idx_sem,
    q_ssem,
    q_rsem,
    m_ssem,
    m_rsem,
    l_ssem,
    l_rsem,
    p_ssem,
    p_rsem,
):
    me = lax.axis_index("dp")
    my_t = lax.axis_index("tensor")
    my_z, my_x = lax.div(me, NX), lax.rem(me, NX)

    def partner(dz, dx):
        return lax.rem(my_z + dz, NZ) * NX + lax.rem(my_x + dx, NX)

    barrier = pltpu.get_barrier_semaphore()

    def greet(offset, carry):
        other = lax.rem(me + offset, NZ * NX)
        pl.semaphore_signal(barrier, inc=1, device_id={"dp": other}, device_id_type=MESH)
        return carry

    lax.fori_loop(1, NZ * NX, greet, 0)
    for offset in range(1, NT):
        pl.semaphore_signal(
            barrier,
            inc=1,
            device_id={"tensor": lax.rem(my_t + offset, NT)},
            device_id_type=MESH,
        )

    loads = [
        pltpu.make_async_copy(source, target, load_sem.at[n])
        for n, (source, target) in enumerate(
            [(q_hbm, q_in), (kn_hbm, kn), (vn_hbm, vn), (kc_hbm, kc), (vc_hbm, vc), (res_hbm, res)]
        )
    ]
    for load in loads:
        load.start()

    lane = iota((128, 128), 1)
    row = iota((128, 128), 0)
    owner = jnp.broadcast_to(owner_ref[...], (128, 128))
    dz = lax.rem(lax.div(owner, NX) - my_z + NZ, NZ)
    dx = lax.rem(lax.rem(owner, NX) - my_x + NX, NX)
    group = jnp.where(dz < NZ // 2, NZ - 1 - 2 * dz, 2 * dz - NZ)
    pair_lane = jnp.where(lane < CANDS, group * NX + dx, 1000 + lane)
    pair_row = pair_lane.T
    same = pair_lane == pair_row
    rank_lane = jnp.sum(jnp.where(same & (row < lane), 1, 0), axis=0, keepdims=True)
    rank_row = jnp.sum(jnp.where(same & (lane < row), 1, 0), axis=1, keepdims=True)
    slot_lane = pair_lane * RANKS + rank_lane
    slot_row = pair_row * RANKS + rank_row
    place[...] = jnp.where(row == slot_lane, 1.0, 0.0).astype(jnp.bfloat16)
    chosen = jnp.sum(jnp.where(slot_row == lane, row, 0), axis=0, keepdims=True)
    idx_v[...] = jnp.broadcast_to(chosen, (8, 128))
    fetch = pltpu.make_async_copy(idx_v, idx_s, idx_sem)
    fetch.start()

    to_row = iota((256, 256), 0)
    from_row = iota((256, 256), 1)
    source_row = (to_row // ROWS) * ROWS + (to_row % LENGTH) * HEADS + (to_row % ROWS) // LENGTH
    shuffle = jnp.where(from_row == source_row, 1.0, 0.0).astype(jnp.bfloat16)
    loads[0].wait()

    def reorder(n, carry):
        rows = q_in[pl.ds(n * 8, 8)].reshape(256, HD)
        mixed = jnp.dot(shuffle, rows, preferred_element_type=jnp.float32)
        q_perm[pl.ds(n * 8, 8)] = mixed.astype(jnp.bfloat16).reshape(8, ROWS, HD)
        return carry

    lax.fori_loop(0, CANDS // 8, reorder, 0)
    fetch.wait()

    def pack(group, carry):
        for n in range(PAIR):
            slot = group * PAIR + n
            q_out[slot] = q_perm[idx_s[0, slot]]
        return carry

    lax.fori_loop(0, GROUPS, pack, 0)

    pl.semaphore_wait(barrier, NZ * NX - 1 + NT - 1)

    def span(ref, group, dx, per):
        return ref.at[pl.ds((group * NX + dx) * per, per)]

    def remote(source, target, ssem, rsem, group, dx, per, forth):
        dz = group_dz(group)
        to = partner(dz, dx) if forth else partner(NZ - dz, NX - dx)
        return pltpu.make_async_remote_copy(
            src_ref=span(source, group, dx, per),
            dst_ref=span(target, group, dx, per),
            send_sem=ssem.at[group],
            recv_sem=rsem.at[group],
            device_id={"dp": to},
            device_id_type=MESH,
        )

    last = GROUPS - 1

    def keep(source, target, rsem, per):
        return pltpu.make_async_copy(
            span(source, last, 0, per), span(target, last, 0, per), rsem.at[last]
        )

    def send(source, target, ssem, rsem, group, per, forth):
        for dx in range(1, NX):
            remote(source, target, ssem, rsem, group, dx, per, forth).start()

        @pl.when(group != last)
        def _():
            remote(source, target, ssem, rsem, group, 0, per, forth).start()

        @pl.when(group == last)
        def _():
            keep(source, target, rsem, per).start()

    def arrived(target, rsem, group, per):
        whole = target.at[pl.ds(group * NX * per, NX * per)]
        pltpu.make_async_copy(whole, whole, rsem.at[group]).wait()

    def send_query(n, carry):
        group = lax.rem(n + last, GROUPS)
        send(q_out, q_got, q_ssem, q_rsem, group, RANKS, True)
        return carry

    lax.fori_loop(0, GROUPS, send_query, 0)

    scale = LOG2E / math.sqrt(HD)

    def softmax_values(scores, value_rows):
        highest = jnp.max(scores, axis=1, keepdims=True)
        powers = jnp.exp2(scores - highest)
        total = jnp.sum(powers, axis=1, keepdims=True)
        sums = jnp.dot(powers.astype(jnp.bfloat16), value_rows, preferred_element_type=jnp.float32)
        return sums / total, highest + jnp.log2(total)

    def scores_of(query_rows, key_rows):
        return (
            lax.dot_general(
                query_rows, key_rows, (((1,), (1,)), ((), ())), preferred_element_type=jnp.float32
            )
            * scale
        )

    loads[1].wait()
    loads[2].wait()
    at_row = iota((512, 128), 0)
    at_key = iota((512, 128), 1)
    seen = (at_row // ROWS == at_key // LENGTH) & (at_key % LENGTH <= at_row % LENGTH)

    def own_tokens(n, carry):
        rows = q_perm[pl.ds(n * 16, 16)].reshape(512, HD)
        scores = scores_of(rows, kn[pl.ds(n * 128, 128)])
        scores = jnp.where(seen, scores, MASKED)
        averages, logs = softmax_values(scores, vn[pl.ds(n * 128, 128)])
        own_o[pl.ds(n * 16, 16)] = averages.reshape(16, ROWS, HD)
        own_l[pl.ds(n * 16, 16)] = jnp.broadcast_to(logs, (512, HD)).reshape(16, ROWS, HD)
        return carry

    lax.fori_loop(0, CANDS // 16, own_tokens, 0)

    loads[3].wait()
    loads[4].wait()
    bias[...] = jnp.where(iota((8, PMAX), 1) < plen_ref[0], 0.0, MASKED)
    spread = iota((256, 128), 0) % (RANKS * ROWS) == iota((256, 128), 1)

    def prefix(n, carry):
        group = lax.rem(n + last, GROUPS)
        arrived(q_got, q_rsem, group, RANKS)
        rows = q_got[pl.ds(group * PAIR, PAIR)].reshape(256, HD)
        scores = scores_of(rows, kc[...]) + bias[0:1, :]
        averages, logs = softmax_values(scores, vc[...])
        m_out[pl.ds(group * PAIR, PAIR)] = averages.astype(jnp.bfloat16).reshape(PAIR, ROWS, HD)
        packed = jnp.where(spread, logs, 0.0).reshape(NX, RANKS * ROWS, HD)
        l_out[pl.ds(group * NX, NX)] = jnp.sum(packed, axis=1, keepdims=True)
        send(m_out, m_got, m_ssem, m_rsem, group, RANKS, False)
        send(l_out, l_got, l_ssem, l_rsem, group, 1, False)
        return carry

    lax.fori_loop(0, GROUPS, prefix, 0)

    loads[5].wait()
    acc[...] = jnp.zeros_like(acc)
    slot_lane8 = iota((LENGTH, 128), 1)

    def finish(n, carry):
        group = lax.rem(n + last, GROUPS)
        arrived(m_got, m_rsem, group, RANKS)
        arrived(l_got, l_rsem, group, 1)
        logs = jnp.broadcast_to(l_got[pl.ds(group * NX, NX)], (NX, RANKS * ROWS, HD))
        logs = jnp.where(spread, logs.reshape(256, HD), 0.0)
        logs = jnp.sum(logs, axis=1, keepdims=True).reshape(PAIR, ROWS, 1)
        squares, dots = acc[0], acc[1]
        for n in range(PAIR):
            slot = group * PAIR + n
            cand = idx_s[0, slot]
            far_log = jnp.broadcast_to(logs[n], (ROWS, HD))
            near_log = own_l[cand]
            top = jnp.maximum(far_log, near_log)
            far, near = jnp.exp2(far_log - top), jnp.exp2(near_log - top)
            mixed = (far * m_got[slot].astype(jnp.float32) + near * own_o[cand]) / (far + near)
            stream = res[cand].astype(jnp.float32)
            square = jnp.zeros((LENGTH, HD), jnp.float32)
            dot = jnp.zeros((LENGTH, HD), jnp.float32)
            for head in range(HEADS):
                hidden = (
                    stream[:, head * HD : (head + 1) * HD]
                    + mixed[head * LENGTH : (head + 1) * LENGTH]
                )
                square += hidden * hidden
                dot += hidden * weight_ref[head : head + 1, :]
            here = slot_lane8 == slot
            squares += jnp.where(here, jnp.sum(square, axis=1, keepdims=True), 0.0)
            dots += jnp.where(here, jnp.sum(dot, axis=1, keepdims=True), 0.0)
        acc[0], acc[1] = squares, dots
        return carry

    lax.fori_loop(0, GROUPS, finish, 0)

    part[my_t] = acc[...]
    shares = []
    for offset in range(1, NT):
        shares.append(
            pltpu.make_async_remote_copy(
                src_ref=acc,
                dst_ref=part.at[my_t],
                send_sem=p_ssem.at[offset],
                recv_sem=p_rsem.at[offset],
                device_id={"tensor": lax.rem(my_t + offset, NT)},
                device_id_type=MESH,
            )
        )
        shares[-1].start()
    for share in shares:
        share.wait_recv()
    total = part[0]
    for n in range(1, NT):
        total += part[n]
    scored = total[1] * lax.rsqrt(total[0] / FEATURES + EPSILON)
    result = jnp.zeros((LENGTH, 128), jnp.float32)
    for _ in range(3):
        piece = scored.astype(jnp.bfloat16)
        scored = scored - piece.astype(jnp.float32)
        result += jnp.dot(piece, place[...], preferred_element_type=jnp.float32)
    inside = iota((LENGTH, 128), 0) < len_ref[...]
    out_ref[...] = jnp.where(inside, result, 0.0)[:, :CANDS]

    for share in shares:
        share.wait_send()

    def sent(source, ssem, group, per, blocks):
        whole = source.at[pl.ds(group * NX * per, blocks * per)]
        pltpu.make_async_copy(whole, whole, ssem.at[group]).wait()

    def drain(group, carry):
        sent(q_out, q_ssem, group, RANKS, NX)
        sent(m_out, m_ssem, group, RANKS, NX)
        sent(l_out, l_ssem, group, 1, NX)
        return carry

    lax.fori_loop(0, last, drain, 0)
    sent(q_out, q_ssem, last, RANKS, NX - 1)
    sent(m_out, m_ssem, last, RANKS, NX - 1)
    sent(l_out, l_ssem, last, 1, NX - 1)


def body(
    queries,
    keys_new,
    values_new,
    residual,
    cand_len,
    owner_map,
    prompt_len,
    keys_cache,
    values_cache,
    norm_gain,
    value_head,
):
    bf16, f32 = jnp.bfloat16, jnp.float32
    weight = (norm_gain.astype(f32) * value_head.astype(f32)).reshape(HEADS, HD)
    vmem = pl.BlockSpec(memory_space=pltpu.VMEM)
    hbm = pl.BlockSpec(memory_space=pl.ANY)
    slots = pltpu.VMEM((SLOTS, ROWS, HD), bf16)
    logs = pltpu.VMEM((GROUPS * NX, 1, HD), f32)
    by_group = pltpu.SemaphoreType.DMA((GROUPS,))
    by_offset = pltpu.SemaphoreType.DMA((NT,))
    scored = pl.pallas_call(
        kernel,
        out_shape=jax.ShapeDtypeStruct((LENGTH, CANDS), f32),
        in_specs=[vmem, vmem, vmem, pl.BlockSpec(memory_space=pltpu.SMEM)] + [hbm] * 6,
        out_specs=vmem,
        scratch_shapes=[
            pltpu.VMEM((CANDS, ROWS, HD), bf16),
            pltpu.VMEM((CANDS * LENGTH, HD), bf16),
            pltpu.VMEM((CANDS * LENGTH, HD), bf16),
            pltpu.VMEM((CANDS, LENGTH, HEADS * HD), bf16),
            pltpu.VMEM((PMAX, HD), bf16),
            pltpu.VMEM((PMAX, HD), bf16),
            pltpu.VMEM((CANDS, ROWS, HD), bf16),
            slots,
            slots,
            slots,
            slots,
            logs,
            logs,
            pltpu.VMEM((CANDS, ROWS, HD), f32),
            pltpu.VMEM((CANDS, ROWS, HD), f32),
            pltpu.VMEM((8, PMAX), f32),
            pltpu.VMEM((8, 128), jnp.int32),
            pltpu.SMEM((8, 128), jnp.int32),
            pltpu.VMEM((128, 128), bf16),
            pltpu.VMEM((2, LENGTH, 128), f32),
            pltpu.VMEM((NT, 2, LENGTH, 128), f32),
            pltpu.SemaphoreType.DMA((6,)),
            pltpu.SemaphoreType.DMA,
            by_group,
            by_group,
            by_group,
            by_group,
            by_group,
            by_group,
            by_offset,
            by_offset,
        ],
        compiler_params=pltpu.CompilerParams(
            collective_id=0, has_side_effects=True, vmem_limit_bytes=40 * 2**20
        ),
    )(
        jnp.pad(owner_map, (0, 128 - CANDS)).reshape(1, 128),
        jnp.pad(cand_len, (0, 128 - CANDS)).reshape(1, 128),
        weight,
        prompt_len,
        queries.reshape(CANDS, ROWS, HD),
        keys_new.reshape(CANDS * LENGTH, HD),
        values_new.reshape(CANDS * LENGTH, HD),
        residual,
        keys_cache.reshape(PMAX, HD),
        values_cache.reshape(PMAX, HD),
    )
    return scored.T


def solution(mesh):
    in_specs = (
        P("dp", None, "tensor", None),
        P("dp", None, "tensor", None),
        P("dp", None, "tensor", None),
        P("dp", None, "tensor"),
        P("dp"),
        P("dp"),
        P("dp"),
        P("dp", None, "tensor", None),
        P("dp", None, "tensor", None),
        P("tensor"),
        P("tensor"),
    )
    out_specs = P("dp", None)
    return jax.shard_map(body, mesh=mesh, in_specs=in_specs, out_specs=out_specs, check_vma=False)
```

time: 261 us -> 128 us (0.49)
  the two profiles are of different devices: /device:TPU:2 before, /device:TPU:1 now
where the time goes in v1:
time: 128 us; the launch traced here: 127 us
  Pallas kernels  119 us (93%)
  local copies, waits for them, and re-layouts  7.92 us (6%)
    pallas_call x1, Pallas kernels, body(): pl.pallas_call(kernel, out_shape=jax.ShapeDtypeStruct((LENGTH, CANDS), f3...  119 us
    unnamed x21, local copies, waits for them, and re-layouts  7.92 us

profile of v1, /device:TPU:1, one launch (start us, length us, event | category | flops | bytes accessed | tf_op | source)
XLA Modules:
  0.0 127.5 jit_solution(7420585461954339430)
XLA Ops:
  0.7 0.0 copy-start.8
  0.7 0.0 copy-start.9
  0.7 0.6 copy-done.8
  1.3 0.0 copy-done.9
  1.3 0.0 copy-start.7
  1.3 0.0 copy-start.6
  1.3 0.7 copy-done.7
  2.0 0.0 copy-done.6
  2.0 0.0 copy-start
  2.0 1.0 copy-done
  3.1 0.0 copy-start.1
  3.1 1.0 copy-done.1
  4.1 0.0 copy-start.2
  4.1 1.0 copy-done.2
  5.2 0.0 copy-start.3
  5.2 1.0 copy-done.3
  6.2 0.0 copy-start.4
  6.2 0.9 copy-done.4
  7.1 0.0 copy-start.5
  7.1 0.9 copy-done.5
  8.0 118.8 %shard_map.109 = f32[8,64]{1,0:T(8,128)S(1)} custom-call(s32[1,128]{1,0:T(1,128)S(1)} %get-tuple-element.6.owner_ref, s32[1,128]{1,0:T(1,128)S(1)} %get-tuple-element.5.len_ref, f32[4,128]{1,0:T(4,128)S(1)} %multiply_bitcast_fusion.weight_ref, s32[1]{0:T(128)S(6)} %copy.13.plen_ref, bf16[64,32,128]{2,1,0:T(8,128)(2,1)S(1)} %bitcast.12, ...), custom_call_target="tpu_custom_call" | custom-call | tf_op jit(solution)/shard_map/pallas_call | solution.py:365
  126.9 0.6 copy.14
  (2 shorter events, 0.0 us)
Async XLA Ops:
  0.7 0.7 copy-start.8
  0.7 0.7 copy-start.9
  1.3 0.7 copy-start.7
  1.3 0.7 copy-start.6
  2.0 1.0 copy-start
  3.1 1.0 copy-start.1
  4.1 1.0 copy-start.2
  5.2 1.0 copy-start.3
  6.2 0.9 copy-start.4
  7.1 0.9 copy-start.5

commit v2 on v1

--- a/solution.py
+++ b/solution.py
@@ -14,6 +14,8 @@
 NX = 4
 NT = 8
 RANKS = 2
+HALF = NZ // 2
+LEAD = 4
 GROUPS = NZ
 PAIR = NX * RANKS
 SLOTS = GROUPS * PAIR
@@ -32,16 +34,24 @@
     return lax.broadcasted_iota(jnp.int32, shape, dim)
 
 
-def group_dz(group):
-    size = 8 - (group + 1) // 2
-    return lax.rem(NZ + (2 * lax.rem(group, 2) - 1) * size, NZ)
+def send_order(step):
+    return jnp.where(lax.rem(step, 2) == 0, HALF - step // 2, lax.rem(NZ - step // 2, NZ))
+
+
+def source_of(step, z):
+    middle = step - LEAD
+    later = jnp.where(step < LEAD, 0, jnp.where(step < GROUPS - LEAD, lax.rem(middle + GROUPS, 2), 1))
+    turn = jnp.where(later == 0, LEAD + middle // 2, middle // 2)
+    turn = jnp.where(step < LEAD, step, jnp.where(step < GROUPS - LEAD, turn, step - HALF))
+    return later * HALF + lax.rem(z + turn, HALF)
 
 
 def kernel(
-    owner_ref,
-    len_ref,
-    weight_ref,
     plen_ref,
+    owner_hbm,
+    len_hbm,
+    gain_hbm,
+    head_hbm,
     q_hbm,
     kn_hbm,
     vn_hbm,
@@ -49,6 +59,10 @@
     kc_hbm,
     vc_hbm,
     out_ref,
+    owner_ref,
+    len_ref,
+    gain_ref,
+    head_ref,
     q_in,
     kn,
     vn,
@@ -88,6 +102,26 @@
     def partner(dz, dx):
         return lax.rem(my_z + dz, NZ) * NX + lax.rem(my_x + dx, NX)
 
+    loads = [
+        pltpu.make_async_copy(source, target, load_sem.at[n])
+        for n, (source, target) in enumerate(
+            [
+                (owner_hbm, owner_ref),
+                (q_hbm, q_in),
+                (kn_hbm, kn),
+                (vn_hbm, vn),
+                (kc_hbm, kc),
+                (vc_hbm, vc),
+                (res_hbm, res),
+                (len_hbm, len_ref),
+                (gain_hbm, gain_ref),
+                (head_hbm, head_ref),
+            ]
+        )
+    ]
+    for load in loads:
+        load.start()
+
     barrier = pltpu.get_barrier_semaphore()
 
     def greet(offset, carry):
@@ -104,30 +138,22 @@
             device_id_type=MESH,
         )
 
-    loads = [
-        pltpu.make_async_copy(source, target, load_sem.at[n])
-        for n, (source, target) in enumerate(
-            [(q_hbm, q_in), (kn_hbm, kn), (vn_hbm, vn), (kc_hbm, kc), (vc_hbm, vc), (res_hbm, res)]
-        )
-    ]
-    for load in loads:
-        load.start()
-
-    lane = iota((128, 128), 1)
-    row = iota((128, 128), 0)
-    owner = jnp.broadcast_to(owner_ref[...], (128, 128))
+    loads[0].wait()
+    lane = iota((CANDS, CANDS), 1)
+    row = iota((CANDS, CANDS), 0)
+    owner = jnp.broadcast_to(owner_ref[...], (CANDS, CANDS))
     dz = lax.rem(lax.div(owner, NX) - my_z + NZ, NZ)
     dx = lax.rem(lax.rem(owner, NX) - my_x + NX, NX)
-    group = jnp.where(dz < NZ // 2, NZ - 1 - 2 * dz, 2 * dz - NZ)
-    pair_lane = jnp.where(lane < CANDS, group * NX + dx, 1000 + lane)
+    pair_lane = dz * NX + dx
     pair_row = pair_lane.T
     same = pair_lane == pair_row
     rank_lane = jnp.sum(jnp.where(same & (row < lane), 1, 0), axis=0, keepdims=True)
     rank_row = jnp.sum(jnp.where(same & (lane < row), 1, 0), axis=1, keepdims=True)
-    slot_lane = pair_lane * RANKS + rank_lane
-    slot_row = pair_row * RANKS + rank_row
-    place[...] = jnp.where(row == slot_lane, 1.0, 0.0).astype(jnp.bfloat16)
-    chosen = jnp.sum(jnp.where(slot_row == lane, row, 0), axis=0, keepdims=True)
+    slot_lane = pair_lane[0:1] * RANKS + rank_lane
+    slot_row = pair_row[:, 0:1] * RANKS + rank_row
+    place[...] = jnp.where(iota((SLOTS, CANDS), 0) == slot_lane, 1.0, 0.0).astype(jnp.bfloat16)
+    held = jnp.where(slot_row == iota((CANDS, SLOTS), 1), iota((CANDS, SLOTS), 0), 0)
+    chosen = jnp.sum(held, axis=0, keepdims=True)
     idx_v[...] = jnp.broadcast_to(chosen, (8, 128))
     fetch = pltpu.make_async_copy(idx_v, idx_s, idx_sem)
     fetch.start()
@@ -136,7 +162,7 @@
     from_row = iota((256, 256), 1)
     source_row = (to_row // ROWS) * ROWS + (to_row % LENGTH) * HEADS + (to_row % ROWS) // LENGTH
     shuffle = jnp.where(from_row == source_row, 1.0, 0.0).astype(jnp.bfloat16)
-    loads[0].wait()
+    loads[1].wait()
 
     def reorder(n, carry):
         rows = q_in[pl.ds(n * 8, 8)].reshape(256, HD)
@@ -147,22 +173,13 @@
     lax.fori_loop(0, CANDS // 8, reorder, 0)
     fetch.wait()
 
-    def pack(group, carry):
-        for n in range(PAIR):
-            slot = group * PAIR + n
-            q_out[slot] = q_perm[idx_s[0, slot]]
-        return carry
-
-    lax.fori_loop(0, GROUPS, pack, 0)
-
     pl.semaphore_wait(barrier, NZ * NX - 1 + NT - 1)
 
     def span(ref, group, dx, per):
         return ref.at[pl.ds((group * NX + dx) * per, per)]
 
     def remote(source, target, ssem, rsem, group, dx, per, forth):
-        dz = group_dz(group)
-        to = partner(dz, dx) if forth else partner(NZ - dz, NX - dx)
+        to = partner(group, dx) if forth else partner(NZ - group, NX - dx)
         return pltpu.make_async_remote_copy(
             src_ref=span(source, group, dx, per),
             dst_ref=span(target, group, dx, per),
@@ -172,22 +189,20 @@
             device_id_type=MESH,
         )
 
-    last = GROUPS - 1
-
     def keep(source, target, rsem, per):
         return pltpu.make_async_copy(
-            span(source, last, 0, per), span(target, last, 0, per), rsem.at[last]
+            span(source, 0, 0, per), span(target, 0, 0, per), rsem.at[0]
         )
 
     def send(source, target, ssem, rsem, group, per, forth):
         for dx in range(1, NX):
             remote(source, target, ssem, rsem, group, dx, per, forth).start()
 
-        @pl.when(group != last)
+        @pl.when(group != 0)
         def _():
             remote(source, target, ssem, rsem, group, 0, per, forth).start()
 
-        @pl.when(group == last)
+        @pl.when(group == 0)
         def _():
             keep(source, target, rsem, per).start()
 
@@ -195,12 +210,17 @@
         whole = target.at[pl.ds(group * NX * per, NX * per)]
         pltpu.make_async_copy(whole, whole, rsem.at[group]).wait()
 
-    def send_query(n, carry):
-        group = lax.rem(n + last, GROUPS)
+    def send_query(group):
+        for n in range(PAIR):
+            slot = group * PAIR + n
+            q_out[slot] = q_perm[idx_s[0, slot]]
         send(q_out, q_got, q_ssem, q_rsem, group, RANKS, True)
-        return carry
-
-    lax.fori_loop(0, GROUPS, send_query, 0)
+
+    def send_first(step, carry):
+        send_query(send_order(step))
+        return carry
+
+    lax.fori_loop(0, GROUPS, send_first, 0)
 
     scale = LOG2E / math.sqrt(HD)
 
@@ -219,8 +239,8 @@
             * scale
         )
 
-    loads[1].wait()
     loads[2].wait()
+    loads[3].wait()
     at_row = iota((512, 128), 0)
     at_key = iota((512, 128), 1)
     seen = (at_row // ROWS == at_key // LENGTH) & (at_key % LENGTH <= at_row % LENGTH)
@@ -236,13 +256,13 @@
 
     lax.fori_loop(0, CANDS // 16, own_tokens, 0)
 
-    loads[3].wait()
     loads[4].wait()
+    loads[5].wait()
     bias[...] = jnp.where(iota((8, PMAX), 1) < plen_ref[0], 0.0, MASKED)
     spread = iota((256, 128), 0) % (RANKS * ROWS) == iota((256, 128), 1)
 
-    def prefix(n, carry):
-        group = lax.rem(n + last, GROUPS)
+    def prefix(step, carry):
+        group = lax.rem(my_z - source_of(step, my_z) + NZ, NZ)
         arrived(q_got, q_rsem, group, RANKS)
         rows = q_got[pl.ds(group * PAIR, PAIR)].reshape(256, HD)
         scores = scores_of(rows, kc[...]) + bias[0:1, :]
@@ -256,12 +276,14 @@
 
     lax.fori_loop(0, GROUPS, prefix, 0)
 
-    loads[5].wait()
+    for load in loads[6:]:
+        load.wait()
+    weight = gain_ref[...].astype(jnp.float32) * head_ref[...].astype(jnp.float32)
     acc[...] = jnp.zeros_like(acc)
     slot_lane8 = iota((LENGTH, 128), 1)
 
-    def finish(n, carry):
-        group = lax.rem(n + last, GROUPS)
+    def finish(step, carry):
+        group = send_order(step)
         arrived(m_got, m_rsem, group, RANKS)
         arrived(l_got, l_rsem, group, 1)
         logs = jnp.broadcast_to(l_got[pl.ds(group * NX, NX)], (NX, RANKS * ROWS, HD))
@@ -285,7 +307,7 @@
                     + mixed[head * LENGTH : (head + 1) * LENGTH]
                 )
                 square += hidden * hidden
-                dot += hidden * weight_ref[head : head + 1, :]
+                dot += hidden * weight[head : head + 1, :]
             here = slot_lane8 == slot
             squares += jnp.where(here, jnp.sum(square, axis=1, keepdims=True), 0.0)
             dots += jnp.where(here, jnp.sum(dot, axis=1, keepdims=True), 0.0)
@@ -314,13 +336,13 @@
     for n in range(1, NT):
         total += part[n]
     scored = total[1] * lax.rsqrt(total[0] / FEATURES + EPSILON)
-    result = jnp.zeros((LENGTH, 128), jnp.float32)
+    result = jnp.zeros((LENGTH, CANDS), jnp.float32)
     for _ in range(3):
         piece = scored.astype(jnp.bfloat16)
         scored = scored - piece.astype(jnp.float32)
         result += jnp.dot(piece, place[...], preferred_element_type=jnp.float32)
-    inside = iota((LENGTH, 128), 0) < len_ref[...]
-    out_ref[...] = jnp.where(inside, result, 0.0)[:, :CANDS]
+    inside = iota((LENGTH, CANDS), 0) < len_ref[...]
+    out_ref[...] = jnp.where(inside, result, 0.0)
 
     for share in shares:
         share.wait_send()
@@ -335,10 +357,10 @@
         sent(l_out, l_ssem, group, 1, NX)
         return carry
 
-    lax.fori_loop(0, last, drain, 0)
-    sent(q_out, q_ssem, last, RANKS, NX - 1)
-    sent(m_out, m_ssem, last, RANKS, NX - 1)
-    sent(l_out, l_ssem, last, 1, NX - 1)
+    lax.fori_loop(1, GROUPS, drain, 0)
+    sent(q_out, q_ssem, 0, RANKS, NX - 1)
+    sent(m_out, m_ssem, 0, RANKS, NX - 1)
+    sent(l_out, l_ssem, 0, 1, NX - 1)
 
 
 def body(
@@ -355,7 +377,6 @@
     value_head,
 ):
     bf16, f32 = jnp.bfloat16, jnp.float32
-    weight = (norm_gain.astype(f32) * value_head.astype(f32)).reshape(HEADS, HD)
     vmem = pl.BlockSpec(memory_space=pltpu.VMEM)
     hbm = pl.BlockSpec(memory_space=pl.ANY)
     slots = pltpu.VMEM((SLOTS, ROWS, HD), bf16)
@@ -365,9 +386,13 @@
     scored = pl.pallas_call(
         kernel,
         out_shape=jax.ShapeDtypeStruct((LENGTH, CANDS), f32),
-        in_specs=[vmem, vmem, vmem, pl.BlockSpec(memory_space=pltpu.SMEM)] + [hbm] * 6,
+        in_specs=[pl.BlockSpec(memory_space=pltpu.SMEM)] + [hbm] * 10,
         out_specs=vmem,
         scratch_shapes=[
+            pltpu.VMEM((1, CANDS), jnp.int32),
+            pltpu.VMEM((1, CANDS), jnp.int32),
+            pltpu.VMEM((HEADS, HD), bf16),
+            pltpu.VMEM((HEADS, HD), bf16),
             pltpu.VMEM((CANDS, ROWS, HD), bf16),
             pltpu.VMEM((CANDS * LENGTH, HD), bf16),
             pltpu.VMEM((CANDS * LENGTH, HD), bf16),
@@ -386,10 +411,10 @@
             pltpu.VMEM((8, PMAX), f32),
             pltpu.VMEM((8, 128), jnp.int32),
             pltpu.SMEM((8, 128), jnp.int32),
-            pltpu.VMEM((128, 128), bf16),
+            pltpu.VMEM((SLOTS, CANDS), bf16),
             pltpu.VMEM((2, LENGTH, 128), f32),
             pltpu.VMEM((NT, 2, LENGTH, 128), f32),
-            pltpu.SemaphoreType.DMA((6,)),
+            pltpu.SemaphoreType.DMA((10,)),
             pltpu.SemaphoreType.DMA,
             by_group,
             by_group,
@@ -401,13 +426,14 @@
             by_offset,
         ],
         compiler_params=pltpu.CompilerParams(
-            collective_id=0, has_side_effects=True, vmem_limit_bytes=40 * 2**20
+            collective_id=0, has_side_effects=True, vmem_limit_bytes=62 * 2**20
         ),
     )(
-        jnp.pad(owner_map, (0, 128 - CANDS)).reshape(1, 128),
-        jnp.pad(cand_len, (0, 128 - CANDS)).reshape(1, 128),
-        weight,
         prompt_len,
+        owner_map.reshape(1, CANDS),
+        cand_len.reshape(1, CANDS),
+        norm_gain.reshape(HEADS, HD),
+        value_head.reshape(HEADS, HD),
         queries.reshape(CANDS, ROWS, HD),
         keys_new.reshape(CANDS * LENGTH, HD),
         values_new.reshape(CANDS * LENGTH, HD),

time: 128 us -> 118 us (0.922)
  the two profiles are of different devices: /device:TPU:1 before, /device:TPU:481 now
where the time goes in v2:
time: 118 us; the launch traced here: 117 us
  Pallas kernels  115 us (97%)
  local copies, waits for them, and re-layouts  1.28 us (1%)
    pallas_call x1, Pallas kernels, body(): pl.pallas_call(kernel, out_shape=jax.ShapeDtypeStruct((LENGTH, CANDS), f3...  115 us

profile of v2, /device:TPU:481, one launch (start us, length us, event | category | flops | bytes accessed | tf_op | source)
XLA Modules:
  0.0 117.1 jit_solution(4034624345564784299)
XLA Ops:
  0.7 115.1 %shard_map.109 = f32[8,64]{1,0:T(8,128)} custom-call(s32[1]{0:T(128)S(6)} %copy.13.plen_ref, s32[1,64]{1,0:T(1,128)} %bitcast.18, s32[1,64]{1,0:T(1,128)} %bitcast.19, bf16[4,128]{1,0:T(4,128)(2,1)} %bitcast.16, bf16[4,128]{1,0:T(4,128)(2,1)} %bitcast.17, bf16[64,32,128]{2,1,0:T(8,128)(2,1)} %bitcast.10, bf16[512,128]{1,0:T(8,128)(2,1)} %bitcast.13, ...), custom_call_target="tpu_custom_call" | custom-call | tf_op jit(solution)/shard_map/pallas_call | solution.py:386
  115.8 1.3 %copy.14 = f32[64,8]{0,1:T(8,128)} copy(f32[64,8]{0,1:T(8,128)} %bitcast.15) | data formatting | bytes 4096

commit v3 on v2

--- a/solution.py
+++ b/solution.py
@@ -210,6 +210,10 @@
         whole = target.at[pl.ds(group * NX * per, NX * per)]
         pltpu.make_async_copy(whole, whole, rsem.at[group]).wait()
 
+    def sent(source, ssem, group, per, blocks):
+        whole = source.at[pl.ds(group * NX * per, blocks * per)]
+        pltpu.make_async_copy(whole, whole, ssem.at[group]).wait()
+
     def send_query(group):
         for n in range(PAIR):
             slot = group * PAIR + n
@@ -275,6 +279,13 @@
         return carry
 
     lax.fori_loop(0, GROUPS, prefix, 0)
+
+    def drain_queries(group, carry):
+        sent(q_out, q_ssem, group, RANKS, NX)
+        return carry
+
+    lax.fori_loop(1, GROUPS, drain_queries, 0)
+    sent(q_out, q_ssem, 0, RANKS, NX - 1)
 
     for load in loads[6:]:
         load.wait()
@@ -330,6 +341,16 @@
             )
         )
         shares[-1].start()
+
+    def drain(group, carry):
+        sent(m_out, m_ssem, group, RANKS, NX)
+        sent(l_out, l_ssem, group, 1, NX)
+        return carry
+
+    lax.fori_loop(1, GROUPS, drain, 0)
+    sent(m_out, m_ssem, 0, RANKS, NX - 1)
+    sent(l_out, l_ssem, 0, 1, NX - 1)
+
     for share in shares:
         share.wait_recv()
     total = part[0]
@@ -346,21 +367,6 @@
 
     for share in shares:
         share.wait_send()
-
-    def sent(source, ssem, group, per, blocks):
-        whole = source.at[pl.ds(group * NX * per, blocks * per)]
-        pltpu.make_async_copy(whole, whole, ssem.at[group]).wait()
-
-    def drain(group, carry):
-        sent(q_out, q_ssem, group, RANKS, NX)
-        sent(m_out, m_ssem, group, RANKS, NX)
-        sent(l_out, l_ssem, group, 1, NX)
-        return carry
-
-    lax.fori_loop(1, GROUPS, drain, 0)
-    sent(q_out, q_ssem, 0, RANKS, NX - 1)
-    sent(m_out, m_ssem, 0, RANKS, NX - 1)
-    sent(l_out, l_ssem, 0, 1, NX - 1)
 
 
 def body(

time: 118 us -> 118 us (level)
  no operation moved by 1% of the time
where the time goes in v3:
time: 118 us; the launch traced here: 117 us
  Pallas kernels  115 us (97%)
  local copies, waits for them, and re-layouts  1.28 us (1%)
    pallas_call x1, Pallas kernels, body(): pl.pallas_call(kernel, out_shape=jax.ShapeDtypeStruct((LENGTH, CANDS), f3...  115 us

profile of v3, /device:TPU:481, one launch (start us, length us, event | category | flops | bytes accessed | tf_op | source)
XLA Modules:
  0.0 117.0 jit_solution(15421351201294984075)
XLA Ops:
  0.7 115.0 %shard_map.109 = f32[8,64]{1,0:T(8,128)} custom-call(s32[1]{0:T(128)S(6)} %copy.13.plen_ref, s32[1,64]{1,0:T(1,128)} %bitcast.18, s32[1,64]{1,0:T(1,128)} %bitcast.19, bf16[4,128]{1,0:T(4,128)(2,1)} %bitcast.16, bf16[4,128]{1,0:T(4,128)(2,1)} %bitcast.17, bf16[64,32,128]{2,1,0:T(8,128)(2,1)} %bitcast.10, bf16[512,128]{1,0:T(8,128)(2,1)} %bitcast.13, ...), custom_call_target="tpu_custom_call" | custom-call | tf_op jit(solution)/shard_map/pallas_call | solution.py:392
  115.7 1.3 %copy.14 = f32[64,8]{0,1:T(8,128)} copy(f32[64,8]{0,1:T(8,128)} %bitcast.15) | data formatting | bytes 4096

commit v4 on v3

--- a/solution.py
+++ b/solution.py
@@ -38,12 +38,12 @@
     return jnp.where(lax.rem(step, 2) == 0, HALF - step // 2, lax.rem(NZ - step // 2, NZ))
 
 
-def source_of(step, z):
+def source_of(step, z, way):
     middle = step - LEAD
     later = jnp.where(step < LEAD, 0, jnp.where(step < GROUPS - LEAD, lax.rem(middle + GROUPS, 2), 1))
     turn = jnp.where(later == 0, LEAD + middle // 2, middle // 2)
     turn = jnp.where(step < LEAD, step, jnp.where(step < GROUPS - LEAD, turn, step - HALF))
-    return later * HALF + lax.rem(z + turn, HALF)
+    return later * HALF + lax.rem(z + HALF + way * turn, HALF)
 
 
 def kernel(
@@ -221,7 +221,7 @@
         send(q_out, q_got, q_ssem, q_rsem, group, RANKS, True)
 
     def send_first(step, carry):
-        send_query(send_order(step))
+        send_query(lax.rem(source_of(step, my_z, -1) - my_z + NZ, NZ))
         return carry
 
     lax.fori_loop(0, GROUPS, send_first, 0)
@@ -266,7 +266,7 @@
     spread = iota((256, 128), 0) % (RANKS * ROWS) == iota((256, 128), 1)
 
     def prefix(step, carry):
-        group = lax.rem(my_z - source_of(step, my_z) + NZ, NZ)
+        group = lax.rem(my_z - source_of(step, my_z, 1) + NZ, NZ)
         arrived(q_got, q_rsem, group, RANKS)
         rows = q_got[pl.ds(group * PAIR, PAIR)].reshape(256, HD)
         scores = scores_of(rows, kc[...]) + bias[0:1, :]

time: 118 us -> 121 us (1.025)
  Pallas kernels: 115 us -> 118 us
    pallas_call x1, Pallas kernels: 115 us -> 118 us  [body(): pl.pallas_call(kernel, out_shape=jax.ShapeDtypeStruct((LENGTH, CANDS), f3...]
where the time goes in v4:
time: 121 us; the launch traced here: 120 us
  Pallas kernels  118 us (98%)
  local copies, waits for them, and re-layouts  1.28 us (1%)
    pallas_call x1, Pallas kernels, body(): pl.pallas_call(kernel, out_shape=jax.ShapeDtypeStruct((LENGTH, CANDS), f3...  118 us

profile of v4, /device:TPU:481, one launch (start us, length us, event | category | flops | bytes accessed | tf_op | source)
XLA Modules:
  0.0 120.4 jit_solution(5249916694969696327)
XLA Ops:
  0.7 118.4 %shard_map.109 = f32[8,64]{1,0:T(8,128)} custom-call(s32[1]{0:T(128)S(6)} %copy.13.plen_ref, s32[1,64]{1,0:T(1,128)} %bitcast.18, s32[1,64]{1,0:T(1,128)} %bitcast.19, bf16[4,128]{1,0:T(4,128)(2,1)} %bitcast.16, bf16[4,128]{1,0:T(4,128)(2,1)} %bitcast.17, bf16[64,32,128]{2,1,0:T(8,128)(2,1)} %bitcast.10, bf16[512,128]{1,0:T(8,128)(2,1)} %bitcast.13, ...), custom_call_target="tpu_custom_call" | custom-call | tf_op jit(solution)/shard_map/pallas_call | solution.py:392
  119.1 1.3 %copy.14 = f32[64,8]{0,1:T(8,128)} copy(f32[64,8]{0,1:T(8,128)} %bitcast.15) | data formatting | bytes 4096
